TPU v7x, 256 devices: a whole 4x4x8 slice. The times are simulated.
256 devices in a mesh: ta: 16 (over z, core), wa: 16 (over y, x).
Axes of the slice: x: 4, y: 4, z: 8, core: 2. Of those that a mesh axis runs over, the one named last changes fastest.
Arguments:
- amplitudes: float32 [96, 512, 512], P('wa', 'ta'), may hold values from -6 to 6
- integrals: float32 [96, 512, 32, 512], P('wa', None, 'ta'), may hold values from -0.02734375 to 0.02734375
- blockmap: int32 [96, 32, 8, 8], P('wa', 'ta'), may hold values 0 or 1
- irrep_occ: int32 [96], replicated, may hold values from 0 to 1, as said below
- irrep_virt: int32 [512], replicated, may hold values from 0 to 1, as said below
Outputs:
- cycle_term: float32 [512, 32, 512], P('wa', 'ta')
Inputs may be any that keep to these rules, and one draw needn't show every extreme that they name: `irrep_occ`: labels are constant over each aligned group of 8 occupied orbitals. `irrep_virt`: labels are constant over each aligned block of 64 virtual orbitals.
All inputs are finite; a program needn't handle non-finite values. No bound on the sum of `blockmap` on one device may be relied on, other than what follows from the above.
Results may differ from a plain program's by a relative error of at most 0.00007.
Values sent between devices are 32-bit elements; how exact they have to be, the bound alone decides.
A program may use at most 128 MiB of HBM per device.

v0:
```python
import functools

import jax
import jax.numpy as jnp
from jax import lax
from jax.experimental import pallas as pl
from jax.experimental.pallas import tpu as pltpu
from jax.sharding import PartitionSpec as P

MESH = pl.DeviceIdType.MESH
K = 6
CHIPS = 8
NB = 8
F32 = jnp.float32
BF16 = jnp.bfloat16
LAG = 2
UNITS = 2 * K
DELAY = 1 + 4 * LAG
FAR_RIGHT = (0, 2, 5)
EARLY = (((0, 1), (1, 1)), ((2, 1), (3, 1)), ((4, 1), (0, 2), (5, 1), (1, 2)), ((2, 2), (3, 2)),
         ((0, 3), (4, 2), (5, 2), (1, 3)), ((2, 3), (0, 4), (3, 3), (4, 3), (5, 3), (1, 4)))
LATE = (((2, 4),), ((3, 4),), ((5, 4), (4, 4)), (), (), ())
ROW = 16
SEL = 8 * ROW


def split(v):
    hi = v.astype(BF16)
    lo = (v - hi.astype(F32)).astype(BF16)
    return hi, lo


def kernel(m, s, amp, w, bm, lv, lo_ref, out, A, X, Wf, Vh, Vl, Wh, Wl, bmx, Z, Ch, Cl, accS, acc, RA, RB, RD, S, QD,
           tab, w_sem, x_sem, right_recv, left_recv, sib_recv, ring_send, rs_send, rs_recv):
    t = lax.axis_index("ta")
    wi = lax.axis_index("wa")
    z, h = t // 2, t % 2
    y, x = wi // 4, wi % 4
    mp = m + m % 2
    width = 64 * mp

    def chip(delta):
        return lax.rem(z + delta + CHIPS, CHIPS)

    z_right = {"ta": chip(1) * 2 + h}
    z_left = {"ta": chip(-1) * 2 + h}
    sibling = {"ta": z * 2 + (1 - h)}

    def step(i, delta):
        return lax.rem(i + delta + 4, 4)

    x_next, x_prev = {"wa": y * 4 + step(x, 1)}, {"wa": y * 4 + step(x, -1)}
    y_next, y_prev = {"wa": step(y, 1) * 4 + x}, {"wa": step(y, -1) * 4 + x}
    x_far, y_far = {"wa": y * 4 + step(x, 2)}, {"wa": step(y, 2) * 4 + x}

    own = pltpu.make_async_copy(amp, A, x_sem)
    own.start()

    def w_copy(k):
        return pltpu.make_async_copy(w.at[k], Wf.at[k], w_sem.at[k])

    for k in range(K):
        w_copy(k).start()

    barrier = pltpu.get_barrier_semaphore()
    neighbours = (z_right, z_left, sibling, x_next, x_prev, x_far, y_next, y_prev, y_far)
    for d in neighbours:
        pl.semaphore_signal(barrier, inc=1, device_id=d, device_id_type=MESH)

    labels = [lv[64 * b] for b in range(NB)]
    ones = sum(labels)
    large = jnp.where(ones > NB // 2, 1, 0)
    member = [jnp.where(l == large, 0, 1) for l in labels]
    small_before = [sum(member[:b]) if b else jnp.int32(0) for b in range(NB)]
    rank = [jnp.where(member[b] == 1, small_before[b], b - small_before[b]) for b in range(NB)]
    small = sum(member)
    for g in range(2):
        for i in range(NB):
            for b in range(ROW):
                hit = (member[b] == g) & (rank[b] == i) if i <= b < NB else None
                tab[g * SEL + i * ROW + b] = jnp.int32(0) if hit is None else jnp.where(hit, 1, 0)

    def chosen(g, i, b, shape):
        return jnp.broadcast_to(tab[g * SEL + i * ROW + b], shape) == 1

    def chosen_either(g, lk, i, b, shape):
        one, two = tab[g * SEL + i * ROW + b], tab[(1 - g) * SEL + i * ROW + b]
        return jnp.broadcast_to(one + lk * (two - one), shape) == 1

    def size(g, lk):
        one, two = (NB - small, small) if g == 0 else (small, NB - small)
        return one + lk * (two - one)

    def span(g):
        return NB - (m, s)[g] + 1

    widest = NB - min(m, s) + 1

    def label_of(k):
        return lo_ref[wi * K + k]

    half = lax.broadcasted_iota(jnp.int32, (16, 128), 1) < 64
    own.wait()
    mine = jnp.where(lv[z * 64] == large, 0, 1)

    def pack(k):
        lk = label_of(k)
        group = mine + lk - 2 * mine * lk
        packed = []
        for b in range(NB):
            top, low = A[k, pl.ds(0, 16), pl.ds(b // 2 * 128, 128)], A[k, pl.ds(16, 16), pl.ds(b // 2 * 128, 128)]
            if b % 2:
                top = pltpu.roll(top, 64, 1)
            else:
                low = pltpu.roll(low, 64, 1)
            packed.append(jnp.where(half, top, low))
        for j in range(m):
            value = jnp.zeros((16, 128), F32)
            for b in range(j, min(j + widest, NB)):
                value = jnp.where(chosen_either(0, group, j, b, (16, 128)), packed[b], value)
            X[k, t, pl.ds(16 * j, 16), :] = value

    def unit_copy(u, zz, recv_sem, dest, direction):
        ref = X.at[u, zz * 2 + h]
        return pltpu.make_async_remote_copy(
            src_ref=ref, dst_ref=ref, send_sem=ring_send.at[direction], recv_sem=recv_sem,
            device_id=dest, device_id_type=MESH)

    def to_right(u, zz, d):
        return unit_copy(u, zz, right_recv.at[u * 5 + d], z_right, 0)

    def to_left(u, zz, d):
        return unit_copy(u, zz, left_recv.at[u * 5 + d], z_left, 1)

    def to_sibling(u, zz):
        return unit_copy(u, zz, sib_recv.at[u], sibling, 2)

    def send_own(u, _):
        pack(u)

        @pl.when(u == 0)
        def _():
            pl.semaphore_wait(barrier, len(neighbours))

        to_right(u, z, 1).start()
        to_left(u, z, 1).start()
        to_sibling(u, z).start()
        return 0

    def forward(u, d):
        for side, sign, reach in ((to_right, -1, 4 if u in FAR_RIGHT else 3), (to_left, 1, 3 if u in FAR_RIGHT else 4)):
            if d <= reach:
                side(u, chip(sign * d), d).wait_recv()
                if d < reach:
                    side(u, chip(sign * d), d + 1).start()
                to_sibling(u, chip(sign * d)).start()

    def after(i, moves):
        for j, some in enumerate(moves):
            if some:
                @pl.when(i == j)
                def _():
                    for u, d in some:
                        forward(u, d)

    def w_prep(k):
        w_copy(k).wait()

        def block(i, _):
            for r in range(8):
                bt, j = r // 2, r % 2
                slab = Wf[k, pl.ds(i * 512 + r, 64, stride=8), :]
                mask = bmx[k * 2 + j, i, :, pl.ds(bt * 128, 128)]
                hi, lo = split(slab * jnp.concatenate([mask] * 8, axis=0))
                Vh[k, i, :, pl.ds(r * 128, 128)] = hi
                Vl[k, i, :, pl.ds(r * 128, 128)] = lo
            return 0

        lax.fori_loop(0, NB, block, 0)
        lk = label_of(k)
        for g in range(2):
            def arrange(i, _):
                at = pl.ds(pl.multiple_of((k % 2) * width + i * 64, 64), 64)
                hit = [chosen_either(g, lk, i, i + o, (64, 256)) for o in range(widest)]
                for V, W in ((Vh, Wh), (Vl, Wl)):
                    for c in range(4):
                        value = jnp.zeros((64, 256), BF16)
                        for o in range(widest):
                            value = jnp.where(hit[o], V[k, jnp.minimum(i + o, NB - 1), :, pl.ds(256 * c, 256)], value)
                        W[k // 2, g, at, pl.ds(256 * c, 256)] = value
                return 0

            lax.fori_loop(0, mp, arrange, 0)

    groups = ((0, m, 0), (1, s, 64 * m))

    def build(k):
        ref = X.at[k, pl.ds(0, CHIPS)]
        pltpu.make_async_copy(ref, ref, sib_recv.at[k]).wait()

        for g, count, row0 in groups:
            def unpack(i, _):
                for core in range(2):
                    value = jnp.zeros((16 * m, 128), F32)
                    for o in range(span(g)):
                        b = jnp.minimum(i + o, NB - 1)
                        value = jnp.where(chosen(g, i, i + o, (16 * m, 128)), X[k, 2 * b + core], value)
                    at = row0 + 64 * i + 32 * core
                    for p in range(mp // 2):
                        one = value[32 * p:32 * p + 16]
                        two = value[32 * p + 16:32 * p + 32] if 2 * p + 1 < m else jnp.zeros((16, 128), F32)
                        cols = pl.ds(128 * p, 128)
                        Z[pl.ds(pl.multiple_of(at, 16), 16), cols] = jnp.where(half, one, pltpu.roll(two, 64, 1))
                        Z[pl.ds(pl.multiple_of(at + 16, 16), 16), cols] = jnp.where(half, pltpu.roll(one, 64, 1), two)
                return 0

            lax.fori_loop(0, count, unpack, 0)
        lk = label_of(k)
        into = pl.ds(pl.multiple_of(width * (k % 2), 128), width)
        for g, count, row0 in groups:
            wide = 64 * (count + count % 2)
            big = Z[pl.ds(0, 64 * m), pl.ds(0, wide)]
            few = jnp.concatenate([Z[pl.ds(64 * m, 64 * s), pl.ds(0, wide)]] + [jnp.zeros((64, wide), F32)] * (m - s), axis=0)
            pick = jnp.broadcast_to(lk, (64 * m, wide)) == g
            turned = jnp.where(pick, big, few)
            if mp > m:
                turned = jnp.concatenate([turned, jnp.zeros((64, wide), F32)], axis=0)
            turned = turned.T
            keep = lax.broadcasted_iota(jnp.int32, (64, width), 1) < size(g, lk) * 64
            for i in range(count):
                a = Z[pl.ds(row0 + 64 * i, 64), :]
                c = jnp.where(keep, 2.0 * a - turned[64 * i:64 * i + 64, :], 0.0)
                hi, lo = split(c)
                Ch[k // 2, pl.ds(row0 + 64 * i, 64), into] = hi
                Cl[k // 2, pl.ds(row0 + 64 * i, 64), into] = lo

    def multiply(c):
        n = pl.ds(pl.multiple_of(c * 256, 256), 256)

        def pair(q, _):
            for g, count, row0 in groups:
                rows = pl.ds(row0, 64 * count)
                wh = Wh[q, g, :, n]
                p = jnp.dot(Ch[q, rows, :], wh, preferred_element_type=F32)
                p = p + jnp.dot(Cl[q, rows, :], wh, preferred_element_type=F32)
                p = p + jnp.dot(Ch[q, rows, :], Wl[q, g, :, n], preferred_element_type=F32)
                accS[rows, :] = jnp.where(q == 0, p, accS[rows, :] + p)
            return 0

        lax.fori_loop(0, K // 2, pair, 0)

    def unsort(c):
        cols = pl.ds(pl.multiple_of(256 * c, 256), 256)

        for b in range(NB):
            value = None
            for g, count, row0 in groups:
                for i in range(max(0, b - span(g) + 1), min(b + 1, count)):
                    rows = accS[pl.ds(row0 + 64 * i, 64), :]
                    value = rows if value is None else jnp.where(chosen(g, i, b, (64, 256)), rows, value)
            acc[b // 2, pl.ds(2 * (b % 2), 2), :, cols] = value.reshape(2, 32, 256)

    lax.fori_loop(0, K, send_own, 0)
    lane = lax.broadcasted_iota(jnp.int32, (8, 512), 1) // 64
    row = lax.broadcasted_iota(jnp.int32, (8, 512), 0)
    spread = jnp.where(lane == row, 1.0, 0.0).astype(BF16)
    blocks = jnp.broadcast_to(bm[...].astype(F32).reshape(96, 1, 8), (96, 8, 8)).reshape(768, 8).astype(BF16)
    bmx[...] = jnp.dot(blocks, spread, preferred_element_type=F32).reshape(12, 8, 8, 512)

    accS[...] = jnp.zeros_like(accS)

    def prepare(k, _):
        w_prep(k)
        after(k, EARLY)
        return 0

    lax.fori_loop(0, K, prepare, 0)

    def copy(src, dst, i, dest):
        return pltpu.make_async_remote_copy(
            src_ref=src, dst_ref=dst, send_sem=rs_send.at[i], recv_sem=rs_recv.at[i],
            device_id=dest, device_id_type=MESH)

    along = ((x, x_next, x_prev, x_far), (y, y_next, y_prev, y_far))

    def view(part, c, i, side):
        cols = pl.ds(pl.multiple_of(256 * c + 128 * part, 128), 128)
        two = pl.ds(2 * side, 2)
        return acc.at[two, i, :, cols] if part == 0 else acc.at[i, two, :, cols]

    def first_axis(part, c):
        me, nxt, prv, _ = along[part]
        base = (4 * part + c) * 9
        a, b, d = (r.at[part, c] for r in (RA, RB, RD))
        far, up, down = step(me, 2), step(me, 1), step(me, -1)
        through = [copy(view(part, c, far, 0), a.at[0], base, nxt), copy(view(part, c, far, 1), a.at[1], base + 1, prv)]
        plain = [copy(view(part, c, down, 0), b.at[0], base + 2, prv), copy(view(part, c, up, 1), b.at[1], base + 3, nxt)]
        added = [copy(view(part, c, up, 0), d.at[0], base + 4, nxt), copy(view(part, c, down, 1), d.at[1], base + 5, prv)]
        return through, plain, added

    def second_axis(part, c):
        me, nxt, prv, far = along[1 - part]
        base = (4 * part + c) * 9 + 6
        return [copy(S.at[part, c, step(me, i + 1)], QD.at[part, c, i], base + i, dest)
                for i, dest in enumerate((nxt, far, prv))]

    def begin(c):
        stages = [first_axis(part, c) for part in range(2)]
        for order in range(2):
            for part in range(2):
                for send in stages[part][order]:
                    send.start()

    def middle(c):
        for part in range(2):
            me = along[part][0]
            through, _, added = first_axis(part, c)
            for i in range(2):
                through[i].wait_recv()
                view(part, c, step(me, 1 - 2 * i), i)[...] += RA[part, c, i]
                added[i].start()

    def finish(c):
        for part in range(2):
            me = along[part][0]
            _, plain, added = first_axis(part, c)
            for i in range(2):
                plain[i].wait_recv()
                added[i].wait_recv()
                S[part, c, pl.ds(2 * i, 2)] = view(part, c, me, i)[...] + RB[part, c, i] + RD[part, c, i]
            for send in second_axis(part, c):
                send.start()

    def close(c):
        for part in range(2):
            for send in second_axis(part, c):
                send.wait_recv()
            total = S[part, c, along[1 - part][0]] + QD[part, c, 0] + QD[part, c, 1] + QD[part, c, 2]
            out[:, 2 * c + part, :] = total

    def assemble(k, _):
        build(k)
        after(k, LATE)
        return 0

    lax.fori_loop(0, K, assemble, 0)

    def chunk(c, _):
        @pl.when(c < 4)
        def _():
            multiply(c)
            unsort(c)
            begin(c)

        @pl.when((c >= 1) & (c < 5))
        def _():
            middle(c - 1)

        @pl.when(c >= 2)
        def _():
            finish(c - 2)

        return 0

    lax.fori_loop(0, 6, chunk, 0)
    for c in range(4):
        close(c)

    def drain(c, _):
        for part in range(2):
            for sends in first_axis(part, c) + (second_axis(part, c),):
                for send in sends:
                    send.wait_send()
        return 0

    lax.fori_loop(0, 4, drain, 0)
    for i, ref in enumerate((X.at[pl.ds(0, 3), pl.ds(0, 7)], X.at[pl.ds(0, 3), pl.ds(0, 7)], X.at[:, pl.ds(0, 8)])):
        pltpu.make_async_copy(ref, ref, ring_send.at[i]).wait()


def call(m, s, cid, amplitudes, w, blockmap, irrep_virt, irrep_occ):
    hbm = pl.BlockSpec(memory_space=pl.ANY)
    vmem = pl.BlockSpec(memory_space=pltpu.VMEM)
    smem = pl.BlockSpec(memory_space=pltpu.SMEM)
    DMA = pltpu.SemaphoreType.DMA
    mp = m + m % 2
    rows = 64 * (m + s)
    out = pl.pallas_call(
        functools.partial(kernel, m, s),
        out_shape=jax.ShapeDtypeStruct((32, 8, 128), F32),
        in_specs=[hbm, hbm, vmem, smem, smem],
        out_specs=vmem,
        scratch_shapes=[
            pltpu.VMEM((K, 32, 512), F32),
            pltpu.VMEM((K, 16, 16 * m, 128), F32),
            pltpu.VMEM((K, 4096, 128), F32),
            pltpu.VMEM((K, NB, 64, 1024), BF16),
            pltpu.VMEM((K, NB, 64, 1024), BF16),
            pltpu.VMEM((K // 2, 2, 128 * mp, 1024), BF16),
            pltpu.VMEM((K // 2, 2, 128 * mp, 1024), BF16),
            pltpu.VMEM((12, 8, 8, 512), F32),
            pltpu.VMEM((rows, 64 * mp), F32),
            pltpu.VMEM((K // 2, rows, 128 * mp), BF16),
            pltpu.VMEM((K // 2, rows, 128 * mp), BF16),
            pltpu.VMEM((rows, 256), F32),
            pltpu.VMEM((4, 4, 32, 1024), F32),
            pltpu.VMEM((2, 4, 2, 2, 32, 128), F32),
            pltpu.VMEM((2, 4, 2, 2, 32, 128), F32),
            pltpu.VMEM((2, 4, 2, 2, 32, 128), F32),
            pltpu.VMEM((2, 4, 4, 32, 128), F32),
            pltpu.VMEM((2, 4, 3, 32, 128), F32),
            pltpu.SMEM((2 * SEL,), jnp.int32),
            DMA((K,)),
            DMA,
            DMA((K * 5,)),
            DMA((K * 5,)),
            DMA((K,)),
            DMA((3,)),
            DMA((72,)),
            DMA((72,)),
        ],
        cost_estimate=pl.CostEstimate(flops=10 ** 10, bytes_accessed=14 * 10 ** 6, transcendentals=0),
        compiler_params=pltpu.CompilerParams(
            collective_id=cid, has_side_effects=True, vmem_limit_bytes=60 * 1024 * 1024),
    )(amplitudes, w, blockmap, irrep_virt, irrep_occ)
    return out.reshape(32, 4, 2, 128).transpose(0, 2, 1, 3).reshape(32, 2, 512)


def dense_kernel(amp, w, bm, lv, lo_ref, out, X, Wf, Wh, Wl, bmx, Ch, Cl, acc, RA, RB, RD, S, QA, QB, QD,
           w_sem, x_sem, right_recv, left_recv, sib_recv, ring_send, rs_send, rs_recv):
    t = lax.axis_index("ta")
    wi = lax.axis_index("wa")
    z, h = t // 2, t % 2
    y, x = wi // 4, wi % 4

    def chip(delta):
        return lax.rem(z + delta + CHIPS, CHIPS)

    z_right = {"ta": chip(1) * 2 + h}
    z_left = {"ta": chip(-1) * 2 + h}
    sibling = {"ta": z * 2 + (1 - h)}

    def step(i, delta):
        return lax.rem(i + delta + 4, 4)

    x_next, x_prev = {"wa": y * 4 + step(x, 1)}, {"wa": y * 4 + step(x, -1)}
    y_next, y_prev = {"wa": step(y, 1) * 4 + x}, {"wa": step(y, -1) * 4 + x}

    def rows(zz, hh):
        return pl.ds(pl.multiple_of(zz * 64 + hh * 32, 32), 32)

    own = [
        pltpu.make_async_copy(amp.at[:, :, pl.ds(256 * g, 256)], X.at[:, g, rows(z, h), :], x_sem.at[g])
        for g in range(2)
    ]
    for c in own:
        c.start()

    def w_copy(k):
        return pltpu.make_async_copy(w.at[k], Wf.at[k], w_sem.at[k])

    for k in range(K):
        w_copy(k).start()

    barrier = pltpu.get_barrier_semaphore()
    neighbours = (z_right, z_left, sibling, x_next, x_prev, y_next, y_prev)
    for d in neighbours:
        pl.semaphore_signal(barrier, inc=1, device_id=d, device_id_type=MESH)

    lane = lax.broadcasted_iota(jnp.int32, (8, 512), 1) // 64
    row = lax.broadcasted_iota(jnp.int32, (8, 512), 0)
    spread = jnp.where(lane == row, 1.0, 0.0).astype(BF16)
    blocks = bm[...].astype(F32).reshape(96, 8).astype(BF16)
    bmx[...] = jnp.dot(blocks, spread, preferred_element_type=F32).reshape(12, 8, 512)
    acc[...] = jnp.zeros_like(acc)

    for c in own:
        c.wait()
    pl.semaphore_wait(barrier, len(neighbours))

    def unit_copy(u, zz, recv_sem, dest, direction):
        ref = X.at[u // 2, u % 2, rows(zz, h), :]
        return pltpu.make_async_remote_copy(
            src_ref=ref, dst_ref=ref, send_sem=ring_send.at[direction], recv_sem=recv_sem,
            device_id=dest, device_id_type=MESH)

    def to_right(u, zz, d):
        return unit_copy(u, zz, right_recv.at[u * 5 + d], z_right, 0)

    def to_left(u, zz, d):
        return unit_copy(u, zz, left_recv.at[u * 5 + d], z_left, 1)

    def to_sibling(u, zz):
        return unit_copy(u, zz, sib_recv.at[u // 2], sibling, 2)

    def w_prep(k):
        for r in range(8):
            bt, j = r // 2, r % 2
            for cb in range(8):
                slab = Wf[k, pl.ds(cb * 512 + r, 64, stride=8), :]
                m = bmx[k * 2 + j, pl.ds(cb, 1), pl.ds(bt * 128, 128)]
                hi, lo = split(slab * m)
                Wh[k, pl.ds(cb * 64, 64), pl.ds(r * 128, 128)] = hi
                Wl[k, pl.ds(cb * 64, 64), pl.ds(r * 128, 128)] = lo

    def compute(k, mh):
        lk = lo_ref[wi * K + k]
        blk = lax.broadcasted_iota(jnp.int32, (1, 256), 1) // 64
        for g in range(2):
            labels = jnp.zeros((1, 256), jnp.int32)
            for i in range(4):
                labels = jnp.where(blk == i, lv[(4 * g + i) * 64], labels)
            bt = X[k, mh, pl.ds(256 * g, 256), :].T
            for i in range(4):
                a = X[k, g, pl.ds(pl.multiple_of(256 * mh + 64 * i, 64), 64), :]
                lz = lv[(4 * mh + i) * 64]
                mask = ((labels + (lz + lk)) & 1) == 0
                c = jnp.where(mask, 2.0 * a - bt[64 * i:64 * i + 64, :], 0.0)
                hi, lo = split(c)
                Ch[pl.ds(64 * i, 64), pl.ds(256 * g, 256)] = hi
                Cl[pl.ds(64 * i, 64), pl.ds(256 * g, 256)] = lo
        for nb in range(4):
            n = pl.ds(256 * nb, 256)
            wh = Wh[k, :, n]
            p = jnp.dot(Ch[...], wh, preferred_element_type=F32)
            p = p + jnp.dot(Cl[...], wh, preferred_element_type=F32)
            p = p + jnp.dot(Ch[...], Wl[k, :, n], preferred_element_type=F32)
            acc[pl.ds(2 * mh, 2), :, :, n] += p.reshape(2, 4, 32, 256)

    def tick(s, _):
        @pl.when(s < UNITS)
        def _():
            to_right(s, z, 1).start()
            to_left(s, z, 1).start()
            to_sibling(s, z).start()

        for d in range(1, 5):
            u = s - LAG * d
            inside = (u >= 0) & (u < UNITS)
            even = u % 2 == 0

            @pl.when(inside if d < 4 else inside & even)
            def _():
                zz = chip(-d)
                to_right(u, zz, d).wait_recv()
                if d < 3:
                    to_right(u, zz, d + 1).start()
                elif d == 3:
                    @pl.when(even)
                    def _():
                        to_right(u, zz, d + 1).start()
                to_sibling(u, zz).start()

            @pl.when(inside if d < 4 else inside & jnp.logical_not(even))
            def _():
                zz = chip(d)
                to_left(u, zz, d).wait_recv()
                if d < 3:
                    to_left(u, zz, d + 1).start()
                elif d == 3:
                    @pl.when(jnp.logical_not(even))
                    def _():
                        to_left(u, zz, d + 1).start()
                to_sibling(u, zz).start()

        @pl.when((s >= 1) & (s < 1 + K))
        def _():
            k = s - 1
            w_copy(k).wait()
            w_prep(k)

        v = s - DELAY

        @pl.when((v >= 0) & (v < UNITS))
        def _():
            k, mh = v // 2, v % 2

            @pl.when(mh == 0)
            def _():
                ref = X.at[k, 0]
                pltpu.make_async_copy(ref, ref, sib_recv.at[k]).wait()

            compute(k, mh)

        return 0

    lax.fori_loop(0, UNITS + DELAY, tick, 0)

    def ring_sum(me, nxt, prv, view, bufs, base, result):
        a, b, d = bufs

        def copy(src, dst, i, dest):
            return pltpu.make_async_remote_copy(
                src_ref=src, dst_ref=dst, send_sem=rs_send.at[base + i], recv_sem=rs_recv.at[base + i],
                device_id=dest, device_id_type=MESH)

        first = [
            copy(view(step(me, 2), 0), a.at[0], 0, nxt),
            copy(view(step(me, 2), 1), a.at[1], 1, prv),
            copy(view(step(me, 1), 1), b.at[1], 2, nxt),
            copy(view(step(me, -1), 0), b.at[0], 3, prv),
        ]
        second = [
            copy(view(step(me, 1), 0), d.at[0], 4, nxt),
            copy(view(step(me, -1), 1), d.at[1], 5, prv),
        ]

        def start():
            for c in first:
                c.start()

        def middle():
            for i in range(2):
                first[i].wait_recv()
                ref = view(step(me, 1 if i == 0 else -1), i)
                ref[...] = ref[...] + a[i]
                second[i].start()

        def finish():
            first[2].wait_recv()
            first[3].wait_recv()
            for i in range(2):
                second[i].wait_recv()
                result(i, view(me, i)[...] + b[i] + d[i])

        def drain():
            for c in first + second:
                c.wait_send()

        return start, middle, finish, drain

    def cols(half, i):
        return pl.ds(512 * half + 256 * i, 256)

    def keep(half):
        def result(i, value):
            S[half, i] = value
        return result

    def emit(half):
        def result(i, value):
            for q in range(2):
                out[:, 4 * half + 2 * i + q, :] = value[:, 128 * q:128 * q + 128]
        return result

    def bufs(refs, half):
        return [r.at[half] for r in refs]

    one = [
        ring_sum(x, x_next, x_prev, lambda i, s: acc.at[:, i, :, cols(0, s)], bufs((RA, RB, RD), 0), 0, keep(0)),
        ring_sum(y, y_next, y_prev, lambda i, s: acc.at[i, :, :, cols(1, s)], bufs((RA, RB, RD), 1), 6, keep(1)),
    ]
    two = [
        ring_sum(y, y_next, y_prev, lambda i, s: S.at[0, s, i], bufs((QA, QB, QD), 0), 12, emit(0)),
        ring_sum(x, x_next, x_prev, lambda i, s: S.at[1, s, i], bufs((QA, QB, QD), 1), 18, emit(1)),
    ]
    for p in one:
        p[0]()
    for p in one:
        p[1]()
    for p, q in zip(one, two):
        p[2]()
        q[0]()
    for q in two:
        q[1]()
    for q in two:
        q[2]()
    for p in one + two:
        p[3]()
    for i, ref in enumerate((X.at[:, 0, pl.ds(0, 224), :], X.at[:, 0, pl.ds(0, 224), :], X.at[:, :, pl.ds(0, 256), :])):
        pltpu.make_async_copy(ref, ref, ring_send.at[i]).wait()


def dense_call(cid, amplitudes, w, blockmap, irrep_virt, irrep_occ):
    hbm = pl.BlockSpec(memory_space=pl.ANY)
    vmem = pl.BlockSpec(memory_space=pltpu.VMEM)
    smem = pl.BlockSpec(memory_space=pltpu.SMEM)
    DMA = pltpu.SemaphoreType.DMA
    out = pl.pallas_call(
        dense_kernel,
        out_shape=jax.ShapeDtypeStruct((32, 8, 128), F32),
        in_specs=[hbm, hbm, vmem, smem, smem],
        out_specs=vmem,
        scratch_shapes=[
            pltpu.VMEM((6, 2, 512, 256), F32),
            pltpu.VMEM((6, 4096, 128), F32),
            pltpu.VMEM((6, 512, 1024), BF16),
            pltpu.VMEM((6, 512, 1024), BF16),
            pltpu.VMEM((12, 8, 512), F32),
            pltpu.VMEM((256, 512), BF16),
            pltpu.VMEM((256, 512), BF16),
            pltpu.VMEM((4, 4, 32, 1024), F32),
            pltpu.VMEM((2, 2, 4, 32, 256), F32),
            pltpu.VMEM((2, 2, 4, 32, 256), F32),
            pltpu.VMEM((2, 2, 4, 32, 256), F32),
            pltpu.VMEM((2, 2, 4, 32, 256), F32),
            pltpu.VMEM((2, 2, 32, 256), F32),
            pltpu.VMEM((2, 2, 32, 256), F32),
            pltpu.VMEM((2, 2, 32, 256), F32),
            DMA((6,)),
            DMA((2,)),
            DMA((UNITS * 5,)),
            DMA((UNITS * 5,)),
            DMA((6,)),
            DMA((3,)),
            DMA((24,)),
            DMA((24,)),
        ],
        cost_estimate=pl.CostEstimate(flops=10 ** 10, bytes_accessed=14 * 10 ** 6, transcendentals=0),
        compiler_params=pltpu.CompilerParams(
            collective_id=cid, has_side_effects=True, vmem_limit_bytes=60 * 1024 * 1024),
    )(amplitudes, w, blockmap, irrep_virt, irrep_occ)
    return out.reshape(32, 4, 2, 128).transpose(0, 2, 1, 3).reshape(32, 2, 512)


SIZES = ((4, 4), (5, 3), (6, 2))


def local(amplitudes, integrals, blockmap, irrep_occ, irrep_virt):
    w = integrals.reshape(6, 512, 2, 4, 128).transpose(0, 1, 3, 2, 4).reshape(6, 4096, 128)
    ones = jnp.right_shift(jnp.sum(irrep_virt), 6)
    which = jnp.minimum(jnp.maximum(ones, NB - ones) - 4, len(SIZES))
    branches = [functools.partial(call, m, s, i) for i, (m, s) in enumerate(SIZES)]
    branches.append(functools.partial(dense_call, len(SIZES)))
    return lax.switch(which, branches, amplitudes, w, blockmap, irrep_virt, irrep_occ)


def solution(mesh):
    in_specs = (P("wa", "ta", None), P("wa", None, "ta", None), P("wa", "ta", None, None), P(), P())
    out_specs = P("wa", "ta", None)
    return jax.shard_map(local, mesh=mesh, in_specs=in_specs, out_specs=out_specs, check_vma=False)
```

profile of v0, /device:TPU:2, one launch (start us, length us, event | category | flops | bytes accessed | tf_op | source)
XLA Modules:
  0.0 69.2 jit_solution(3813010565335894274)
XLA Ops:
  0.0 1.3 %reduce_sum.9 = s32[]{:T(128)} reduce(s32[512]{0:T(512)} %param.13, s32[]{:T(128)} %constant.1.clone.1), dimensions={0}, to_apply=%region_0.0 | reduce | flops 511 | bytes 2056 | tf_op jit(solution)/shard_map/reduce_sum | solution.py:721
  2.0 66.5 %conditional.1 = (f32[32,2,512]{2,1,0:T(2,128)S(1)}) conditional(s32[]{:T(128)} %clamp.3, (f32[6,32,512]{2,1,0:T(8,128)}, f32[6,512,4,2,128]{4,3,2,1,0:T(2,128)}, s32[6,2,8,8]{3,2,1,0:T(8,128)}, s32[512]{0:T(512)}, s32[96]{0:T(128)}) %tuple.26, (f32[6,32,512]{2,1,0:T(8,128)}, f32[6,512,4,2,128]{4,3,2,1,0:T(2,128)}, ...), branch_computations={%region_1.0_spmd, %region_2.0_spmd, %region_3.0_spmd, %region_4.0_... | conditional | flops 10000000000 | bytes 14000008 | solution.py:725
  2.0 66.1 %branch_2_fun.1 = f32[32,8,128]{2,1,0:T(8,128)S(1)} custom-call(f32[6,32,512]{2,1,0:T(8,128)} %get-tuple-element.89.amp, f32[6,4096,128]{2,1,0:T(8,128)} %bitcast.37, s32[6,2,8,8]{3,2,1,0:T(8,128)} %get-tuple-element.93.bm, s32[512]{0:T(512)} %get-tuple-element.63.lv, s32[96]{0:T(128)} %get-tuple-element.97.lo_ref), custom_call_target="tpu_custom_call" | custom-call | flops 10000000000 | bytes 14000000 | tf_op jit(solution)/shard_map/cond/branch_2_fun/pallas_call | solution.py:388
  68.5 0.7 copy.27
where the time goes:
time: 69.3 us; the launch traced here: 69.2 us
  Pallas kernels  66.1 us (95%)
  other arithmetic  1.32 us (2%)
    pallas_call x1, Pallas kernels, call(): pl.pallas_call(functools.partial(kernel, m, s), out_shape=jax.ShapeDtypeS...  66.1 us

commit v1 on v0

--- a/solution.py
+++ b/solution.py
@@ -57,7 +57,7 @@
     own.start()
 
     def w_copy(k):
-        return pltpu.make_async_copy(w.at[k], Wf.at[k], w_sem.at[k])
+        return pltpu.make_async_copy(w.at[k], Wf.at[k, pl.ds(0, 4096)], w_sem.at[k])
 
     for k in range(K):
         w_copy(k).start()
@@ -393,7 +393,7 @@
         scratch_shapes=[
             pltpu.VMEM((K, 32, 512), F32),
             pltpu.VMEM((K, 16, 16 * m, 128), F32),
-            pltpu.VMEM((K, 4096, 128), F32),
+            pltpu.VMEM((K, 4104, 128), F32),
             pltpu.VMEM((K, NB, 64, 1024), BF16),
             pltpu.VMEM((K, NB, 64, 1024), BF16),
             pltpu.VMEM((K // 2, 2, 128 * mp, 1024), BF16),
@@ -457,7 +457,7 @@
         c.start()
 
     def w_copy(k):
-        return pltpu.make_async_copy(w.at[k], Wf.at[k], w_sem.at[k])
+        return pltpu.make_async_copy(w.at[k], Wf.at[k, pl.ds(0, 4096)], w_sem.at[k])
 
     for k in range(K):
         w_copy(k).start()
@@ -683,7 +683,7 @@
         out_specs=vmem,
         scratch_shapes=[
             pltpu.VMEM((6, 2, 512, 256), F32),
-            pltpu.VMEM((6, 4096, 128), F32),
+            pltpu.VMEM((6, 4104, 128), F32),
             pltpu.VMEM((6, 512, 1024), BF16),
             pltpu.VMEM((6, 512, 1024), BF16),
             pltpu.VMEM((12, 8, 512), F32),

time: 69.3 us -> 61.5 us (0.89)
  Pallas kernels: 66.1 us -> 58.2 us
    pallas_call x1, Pallas kernels: 66.1 us -> 58.2 us  [call(): pl.pallas_call(functools.partial(kernel, m, s), out_shape=jax.ShapeDtypeS...]
where the time goes in v1:
time: 61.5 us; the launch traced here: 61.1 us
  Pallas kernels  58.2 us (95%)
  other arithmetic  1.32 us (2%)
  between operations  0.67 us (1%)
  local copies, waits for them, and re-layouts  0.66 us (1%)
    pallas_call x1, Pallas kernels, call(): pl.pallas_call(functools.partial(kernel, m, s), out_shape=jax.ShapeDtypeS...  58.2 us
    reduce_sum x1, other arithmetic, local(): ones = jnp.right_shift(jnp.sum(irrep_virt), 6)  1.32 us

profile of v1, /device:TPU:2, one launch (start us, length us, event | category | flops | bytes accessed | tf_op | source)
XLA Modules:
  0.0 61.1 jit_solution(8621940780141384619)
XLA Ops:
  0.0 1.3 %reduce_sum.9 = s32[]{:T(128)} reduce(s32[512]{0:T(512)} %param.13, s32[]{:T(128)} %constant.1.clone.1), dimensions={0}, to_apply=%region_0.0 | reduce | flops 511 | bytes 2056 | tf_op jit(solution)/shard_map/reduce_sum | solution.py:721
  2.0 58.5 %conditional.1 = (f32[32,2,512]{2,1,0:T(2,128)S(1)}) conditional(s32[]{:T(128)} %clamp.3, (f32[6,32,512]{2,1,0:T(8,128)}, f32[6,512,4,2,128]{4,3,2,1,0:T(2,128)}, s32[6,2,8,8]{3,2,1,0:T(8,128)}, s32[512]{0:T(512)}, s32[96]{0:T(128)}) %tuple.26, (f32[6,32,512]{2,1,0:T(8,128)}, f32[6,512,4,2,128]{4,3,2,1,0:T(2,128)}, ...), branch_computations={%region_1.0_spmd, %region_2.0_spmd, %region_3.0_spmd, %region_4.0_... | conditional | flops 10000000000 | bytes 14000008 | solution.py:725
  2.0 58.2 %branch_0_fun.1 = f32[32,8,128]{2,1,0:T(8,128)S(1)} custom-call(f32[6,32,512]{2,1,0:T(8,128)} %get-tuple-element.87.amp, f32[6,4096,128]{2,1,0:T(8,128)} %bitcast.35, s32[6,2,8,8]{3,2,1,0:T(8,128)} %get-tuple-element.91.bm, s32[512]{0:T(512)} %get-tuple-element.53.lv, s32[96]{0:T(128)} %get-tuple-element.95.lo_ref), custom_call_target="tpu_custom_call" | custom-call | flops 10000000000 | bytes 14000000 | tf_op jit(solution)/shard_map/cond/branch_0_fun/pallas_call | solution.py:388
  60.5 0.7 %copy.27 = f32[32,2,512]{2,1,0:T(2,128)} copy(f32[32,2,512]{2,1,0:T(2,128)S(1)} %get-tuple-element.70) | data formatting | bytes 262144
